TPU v7x, 256 devices: a whole 4x4x8 slice. The times are simulated.
256 devices in a mesh: region: 16 (over z, x_lo), neuron: 16 (over x_hi, y, core).
Axes of the slice: x: 4 (x_hi: 2, x_lo: 2; x = x_hi * 2 + x_lo), y: 4, z: 8, core: 2. Of those that a mesh axis runs over, the one named last changes fastest.
Arguments:
- counts: bfloat16 [16, 20480, 4096], P('region', 'neuron'), may hold values from 0 to 3, as said below
- latents: bfloat16 [64, 4096], P(None, 'neuron'), may hold values from -5 to 5
- loadings: bfloat16 [16, 64, 20480], P('region', None, 'neuron'), may hold values from -0.75 to 0.75
- bias: float32 [16, 20480], P('region', 'neuron'), may hold values from -3 to 3
- delays: int32 [16, 64], P('region'), may hold values from 0 to 128
- recorded: int32 [16], P('region'), may hold values from 1024 to 4096, as said below
Outputs:
- grad_latents: float32 [64, 4096], P(None, 'neuron')
- grad_loadings: float32 [16, 64, 20480], P('region', None, 'neuron')
- grad_bias: float32 [16, 20480], P('region', 'neuron')
Inputs may be any that keep to these rules, and one draw needn't show every extreme that they name: At least one region is recorded over all 4096 bins. `counts`: whole numbers.
All inputs are finite; a program needn't handle non-finite values.
Results may differ from a plain program's by a relative error of at most 0.0021.
Values may be sent and summed in bfloat16 or wider, within the bound.
A program may use at most 64 MiB of HBM per device.

v0:
```python
import jax
import jax.numpy as jnp
from jax import lax
from jax.sharding import PartitionSpec as P


def move_rows(source, delay_row, levels, forward):
    current = source
    for level in range(levels):
        amount = 1 << level
        if forward:
            displaced = jnp.pad(current[:, :-amount], ((0, 0), (amount, 0)))
        else:
            displaced = jnp.pad(current[:, amount:], ((0, 0), (0, amount)))
        chosen = delay_row // amount % 2 == 1
        current = jnp.where(chosen[:, None], displaced, current)
    return current


def delay_rows(source, delay_row, offset, span):
    result = move_rows(source, delay_row, offset.bit_length(), True)
    return result[:, offset : offset + span]


def advance_rows(source, delay_row, span, largest):
    result = move_rows(source, delay_row, largest.bit_length(), False)
    return result[:, :span]


def per_device(counts, latents, loadings, bias, delays, recorded):
    count_rows = counts[0]
    load = loadings[0]
    bias_row = bias[0]
    delay_row = delays[0]
    length = recorded[0]
    width = latents.shape[1]
    total = count_rows.shape[1]
    reach = width // 2
    lat_count = latents.shape[0]
    neu_count = count_rows.shape[0]

    def accumulate(carry, piece, start):
        grad_load, grad_bias, grad_shift = carry
        span = piece.shape[1]
        observed = lax.dynamic_slice_in_dim(count_rows, start, span, 1).astype(jnp.float32)
        eta = lax.dot_general(
            load, piece, (((0,), (0,)), ((), ())), preferred_element_type=jnp.float32
        )
        eta = eta + bias_row[:, None]
        bins = start + jnp.arange(span, dtype=jnp.int32)
        resid = jnp.where((bins < length)[None, :], jnp.exp(eta) - observed, 0.0)
        resid_low = resid.astype(jnp.bfloat16)
        grad_load = grad_load + lax.dot_general(
            piece, resid_low, (((1,), (1,)), ((), ())), preferred_element_type=jnp.float32
        )
        grad_bias = grad_bias + jnp.sum(resid, axis=1)
        block = jnp.dot(load, resid_low, preferred_element_type=jnp.float32)
        grad_shift = lax.dynamic_update_slice_in_dim(grad_shift, block, start, 1)
        return (grad_load, grad_bias, grad_shift)

    initial = (
        jnp.zeros((lat_count, neu_count), jnp.float32),
        jnp.zeros((neu_count,), jnp.float32),
        jnp.zeros((lat_count, total), jnp.float32),
    )
    whole = lax.all_gather(latents, "neuron", axis=1, tiled=True)
    shifted = delay_rows(jnp.pad(whole, ((0, 0), (reach, 0))), delay_row, reach, total)

    def visit(step, carry):
        begin = (step * width).astype(jnp.int32)
        return accumulate(carry, lax.dynamic_slice_in_dim(shifted, begin, width, 1), begin)

    grad_load, grad_bias, grad_shift = lax.fori_loop(0, total // width, visit, initial)
    source = advance_rows(jnp.pad(grad_shift, ((0, 0), (0, reach))), delay_row, total, reach)
    summed = lax.psum_scatter(source, "neuron", scatter_dimension=1, tiled=True)
    grad_latents = lax.psum(summed, "region")
    return (grad_latents, grad_load[None], grad_bias[None])


def solution(mesh):
    placed = (
        P("region", "neuron", None),
        P(None, "neuron"),
        P("region", None, "neuron"),
        P("region", "neuron"),
        P("region", None),
        P("region"),
    )
    return jax.shard_map(
        per_device,
        mesh=mesh,
        in_specs=placed,
        out_specs=(P(None, "neuron"), P("region", None, "neuron"), P("region", "neuron")),
        check_vma=False,
    )
```

profile of v0, /device:TPU:8, one launch (start us, length us, event | category | flops | bytes accessed | tf_op | source)
XLA Modules:
  0.0 316.7 jit_solution(13940699881098271327)
XLA Ops:
  7.9 22.8 %all_gather.3 = bf16[64,4096]{1,0:T(8,128)(2,1)S(1)} all-gather(bf16[64,256]{1,0:T(8,128)(2,1)} %param.9), channel_id=1, replica_groups=mesh['region'=16,'neuron'=16] {'neuron'}, dimensions={1}, use_global_device_ids=true | all-gather | bytes 557056 | tf_op jit(solution)/shard_map/all_gather | solution.py:66
  32.7 14.5 %copy.9 = bf16[1,1280,4096]{1,2,0:T(8,128)(2,1)} copy(bf16[1,1280,4096]{2,1,0:T(8,128)(2,1)} %param.8) | data formatting | bytes 20971520 | tf_op args[0]
  47.4 0.7 copy-done.1
  48.1 47.3 %while.18 = (s32[]{:T(128)}, f32[64,1280]{1,0:T(8,128)S(1)}, f32[1280]{0:T(1024)S(1)}, f32[64,4096]{1,0:T(8,128)S(1)}, bf16[64,4096]{1,0:T(8,128)(2,1)S(1)}, /*i...) while((s32[]{:T(128)}, f32[64,1280]{1,0:T(8,128)S(1)}, ...), condition=%wide.region_2.3_spmd.clone, body=%wide.region_0.2_spmd.clone.sunk | while | flops 127960832 | bytes 3776474 | solution.py:73
  48.8 1.6 fusion.44
  51.7 1.6 fusion.44
  54.7 1.6 fusion.44
  57.6 1.6 fusion.44
  60.6 1.6 fusion.44
  63.5 1.6 fusion.44
  66.5 1.6 fusion.44
  69.5 1.6 fusion.44
  72.4 1.6 fusion.44
  75.4 1.6 fusion.44
  78.3 1.6 fusion.44
  81.3 1.6 fusion.44
  84.3 1.6 fusion.44
  87.2 1.6 fusion.44
  90.2 1.6 fusion.44
  93.1 1.6 fusion.44
  99.3 1.2 slice_select_fusion
  100.6 76.1 %reduce-scatter.2.cloned.1.call-done = f32[64,256]{1,0:T(8,128)} async-done(((f32[64,4096]{1,0:T(8,128)}), f32[64,256]{1,0:T(8,128)}) %reduce-scatter.2.cloned.1.call-update) | async-done | bytes 65552 | tf_op jit(solution)/shard_map/reduce_scatter | solution.py:75
  177.3 131.1 %all-reduce.20.cloned.1.call-done = f32[64,256]{1,0:T(8,128)} async-done(((f32[64,256]{1,0:T(8,128)}), f32[64,256]{1,0:T(8,128)}) %all-reduce.20.cloned.1.call-update) | async-done | bytes 65552 | tf_op jit(solution)/shard_map/psum | solution.py:76
  308.4 1.5 copy.24
  (119 shorter events, 27.9 us)
Async XLA Ops:
  7.2 169.5 %reduce-scatter.2.cloned.1.call-start = ((), (), s32[]{:S(2)}) async-start(), calls=%async_computation.1 | async-start | bytes 1114112 | tf_op jit(solution)/shard_map/reduce_scatter | solution.py:75
  47.2 0.9 copy-start.1
  47.2 0.9 copy-start.2
  95.4 0.8 copy-start
  100.6 207.8 %all-reduce.20.cloned.1.call-start = ((), (), s32[]{:S(2)}) async-start(), calls=%async_computation.2 | async-start | bytes 131072 | tf_op jit(solution)/shard_map/psum | solution.py:76
Sparse Core Ops, SparseCore 0:
  100.7 75.9 reduce-scatter.1
  179.5 128.8 all-reduce.19
where the time goes:
time: 318 us; the launch traced here: 317 us
  waiting for transfers between devices  207 us (65%)
  matrix products  35.2 us (11%)
  blocking collectives  22.8 us (7%)
  local copies, waits for them, and re-layouts  20.1 us (6%)
  other arithmetic  16.5 us (5%)
  between operations  14.2 us (4%)
    psum x1, waiting for transfers between devices, per_device(): grad_latents = lax.psum(summed, 'region')  131 us
    reduce_scatter x1, waiting for transfers between devices, per_device(): summed = lax.psum_scatter(source, 'neuron', scatter_dimension=1, tiled=True)  76.1 us
    dot_general x16, matrix products, accumulate(): lax.dot_general(load, piece, (((0,), (0,)), ((), ())), preferred_element_...  26.2 us
    all_gather x1, blocking collectives, per_device(): whole = lax.all_gather(latents, 'neuron', axis=1, tiled=True)  22.8 us
    unnamed x8, local copies, waits for them, and re-layouts  16.9 us
    lt x16, other arithmetic, accumulate(): resid = jnp.where((bins < length)[None, :], jnp.exp(eta) - observed, 0.0)  10.9 us
  transfers between devices with their start and end apart: 2, of which 2 were waited for; matrix products, arithmetic and copies ran while one was open for 0% of the time, Pallas kernels for 0%

commit v1 on v0

--- a/solution.py
+++ b/solution.py
@@ -63,7 +63,15 @@
         jnp.zeros((neu_count,), jnp.float32),
         jnp.zeros((lat_count, total), jnp.float32),
     )
-    whole = lax.all_gather(latents, "neuron", axis=1, tiled=True)
+    whole = jnp.concatenate(
+        lax.all_to_all(
+            jnp.stack([latents] * lax.axis_size("neuron")),
+            axis_name="neuron",
+            split_axis=0,
+            concat_axis=0,
+        ),
+        axis=1,
+    )
     shifted = delay_rows(jnp.pad(whole, ((0, 0), (reach, 0))), delay_row, reach, total)
 
     def visit(step, carry):

time: 318 us -> 305 us (0.959)
  blocking collectives: 22.8 us -> 0 us
  starting transfers between devices: 0.08 us -> 7.47 us
    all_gather x1 -> x0, blocking collectives: 22.8 us -> none  [per_device(): whole = lax.all_gather(latents, 'neuron', axis=1, tiled=True)]
    all_to_all x0 -> x1, starting transfers between devices: none -> 7.39 us  [per_device(): lax.all_to_all(jnp.stack([latents] * lax.axis_size('neuron')), axis_name=...]
    unnamed x8 -> x10, local copies, waits for them, and re-layouts: 16.9 us -> 16.7 us
  transfers between devices with their start and end apart: 2 -> 3, of which waited for: 2 -> 2; matrix products, arithmetic and copies ran while one was open for 0% -> 5% of each run, Pallas kernels for 0% -> 0%
where the time goes in v1:
time: 305 us; the launch traced here: 303 us
  waiting for transfers between devices  208 us (68%)
  matrix products  35.3 us (12%)
  local copies, waits for them, and re-layouts  21.6 us (7%)
  other arithmetic  15.8 us (5%)
  between operations  14.2 us (5%)
  starting transfers between devices  7.47 us (2%)
    psum x1, waiting for transfers between devices, per_device(): grad_latents = lax.psum(summed, 'region')  131 us
    reduce_scatter x1, waiting for transfers between devices, per_device(): summed = lax.psum_scatter(source, 'neuron', scatter_dimension=1, tiled=True)  77 us
    dot_general x16, matrix products, accumulate(): lax.dot_general(load, piece, (((0,), (0,)), ((), ())), preferred_element_...  26.3 us
    unnamed x10, local copies, waits for them, and re-layouts  16.7 us
    lt x16, other arithmetic, accumulate(): resid = jnp.where((bins < length)[None, :], jnp.exp(eta) - observed, 0.0)  10.9 us
    all_to_all x1, starting transfers between devices, per_device(): lax.all_to_all(jnp.stack([latents] * lax.axis_size('neuron')), axis_name=...  7.39 us
  transfers between devices with their start and end apart: 3, of which 2 were waited for; matrix products, arithmetic and copies ran while one was open for 5% of the time, Pallas kernels for 0%

profile of v1, /device:TPU:8, one launch (start us, length us, event | category | flops | bytes accessed | tf_op | source)
XLA Modules:
  0.0 303.1 jit_solution(8787796566576457615)
XLA Ops:
  7.2 1.6 stack.2
  8.8 7.4 %all-to-all-start = ((bf16[16,64,256]{2,1,0:T(8,128)(2,1)}), bf16[16,64,256]{2,1,0:T(8,128)(2,1)S(1)}, u32[]{:S(2)}, u32[]{:S(2)}) async-start(bf16[16,64,256]{2,1,0:T(8,128)(2,1)} %stack.2), calls=%async_computation | async-start | bytes 1048576 | tf_op jit(solution)/shard_map/all_to_all | solution.py:67
  16.2 14.3 %copy.12 = bf16[1,1280,4096]{1,2,0:T(8,128)(2,1)} copy(bf16[1,1280,4096]{2,1,0:T(8,128)(2,1)} %param.8) | data formatting | bytes 20971520 | tf_op args[0]
  33.6 47.4 %while.18 = (s32[]{:T(128)}, f32[64,1280]{1,0:T(8,128)S(1)}, f32[1280]{0:T(1024)S(1)}, f32[64,4096]{1,0:T(8,128)S(1)}, bf16[64,4096]{1,0:T(8,128)(2,1)S(1)}, /*i...) while((s32[]{:T(128)}, f32[64,1280]{1,0:T(8,128)S(1)}, ...), condition=%wide.region_2.3_spmd.clone, body=%wide.region_0.2_spmd.clone.sunk | while | flops 127960832 | bytes 3776474 | solution.py:81
  34.3 1.6 fusion.44
  37.3 1.6 fusion.44
  40.2 1.7 fusion.44
  43.2 1.7 fusion.44
  46.2 1.6 fusion.44
  49.1 1.6 fusion.44
  52.1 1.7 fusion.44
  55.0 1.7 fusion.44
  58.0 1.6 fusion.44
  61.0 1.6 fusion.44
  63.9 1.7 fusion.44
  66.9 1.7 fusion.44
  69.9 1.6 fusion.44
  72.8 1.6 fusion.44
  75.8 1.7 fusion.44
  78.8 1.7 fusion.44
  85.0 1.2 slice_select_fusion
  86.2 77.0 %reduce-scatter.2.cloned.1.call-done = f32[64,256]{1,0:T(8,128)} async-done(((f32[64,4096]{1,0:T(8,128)}), f32[64,256]{1,0:T(8,128)}) %reduce-scatter.2.cloned.1.call-update) | async-done | bytes 65552 | tf_op jit(solution)/shard_map/reduce_scatter | solution.py:83
  163.9 131.0 %all-reduce.20.cloned.1.call-done = f32[64,256]{1,0:T(8,128)} async-done(((f32[64,256]{1,0:T(8,128)}), f32[64,256]{1,0:T(8,128)}) %all-reduce.20.cloned.1.call-update) | async-done | bytes 65552 | tf_op jit(solution)/shard_map/psum | solution.py:84
  294.8 1.5 copy.28
  (124 shorter events, 27.9 us)
Async XLA Ops:
  8.8 21.8 %all-to-all-start = ((bf16[16,64,256]{2,1,0:T(8,128)(2,1)}), bf16[16,64,256]{2,1,0:T(8,128)(2,1)S(1)}, u32[]{:S(2)}, u32[]{:S(2)}) async-start(bf16[16,64,256]{2,1,0:T(8,128)(2,1)} %stack.2), calls=%async_computation | async-start | bytes 1048576 | tf_op jit(solution)/shard_map/all_to_all | solution.py:67
  16.2 147.1 %reduce-scatter.2.cloned.1.call-start = ((), (), s32[]{:S(2)}) async-start(), calls=%async_computation.2 | async-start | bytes 1114112 | tf_op jit(solution)/shard_map/reduce_scatter | solution.py:83
  16.2 14.3 %copy-start.3 = (s32[1,64]{1,0:T(1,128)S(1)}, s32[1,64]{1,0:T(1,128)}, u32[]{:S(2)}) copy-start(s32[1,64]{1,0:T(1,128)} %param.12) | copy-start | bytes 772
  32.7 0.9 copy-start.1
  32.7 0.9 copy-start.2
  81.0 0.8 copy-start
  86.2 208.7 %all-reduce.20.cloned.1.call-start = ((), (), s32[]{:S(2)}) async-start(), calls=%async_computation.3 | async-start | bytes 131072 | tf_op jit(solution)/shard_map/psum | solution.py:84
Sparse Core Ops, SparseCore 0:
  86.3 76.9 reduce-scatter.1
  166.0 128.7 all-reduce.19

commit v2 on v0

--- a/solution.py
+++ b/solution.py
@@ -2,6 +2,11 @@
 import jax.numpy as jnp
 from jax import lax
 from jax.sharding import PartitionSpec as P
+
+
+def summed_here(x, axis):
+    shards = lax.all_gather(x, axis)
+    return jnp.sum(shards, axis=0)
 
 
 def move_rows(source, delay_row, levels, forward):
@@ -73,7 +78,7 @@
     grad_load, grad_bias, grad_shift = lax.fori_loop(0, total // width, visit, initial)
     source = advance_rows(jnp.pad(grad_shift, ((0, 0), (0, reach))), delay_row, total, reach)
     summed = lax.psum_scatter(source, "neuron", scatter_dimension=1, tiled=True)
-    grad_latents = lax.psum(summed, "region")
+    grad_latents = summed_here(summed, "region")
     return (grad_latents, grad_load[None], grad_bias[None])
 
 

time: 318 us -> 257 us (0.81)
  waiting for transfers between devices: 207 us -> 145 us
    psum x1 -> x0, waiting for transfers between devices: 131 us -> none  [per_device(): grad_latents = lax.psum(summed, 'region')]
    all_gather x0 -> x1, waiting for transfers between devices: none -> 69.3 us  [summed_here(): shards = lax.all_gather(x, axis)]
    unnamed x8 -> x7, local copies, waits for them, and re-layouts: 16.9 us -> 15.4 us
where the time goes in v2:
time: 257 us; the launch traced here: 255 us
  waiting for transfers between devices  145 us (56%)
  matrix products  35.2 us (14%)
  blocking collectives  22.8 us (9%)
  local copies, waits for them, and re-layouts  18.6 us (7%)
  other arithmetic  18.4 us (7%)
  between operations  14.2 us (6%)
    reduce_scatter x1, waiting for transfers between devices, per_device(): summed = lax.psum_scatter(source, 'neuron', scatter_dimension=1, tiled=True)  76.1 us
    all_gather x1, waiting for transfers between devices, summed_here(): shards = lax.all_gather(x, axis)  69.3 us
    dot_general x16, matrix products, accumulate(): lax.dot_general(load, piece, (((0,), (0,)), ((), ())), preferred_element_...  26.2 us
    all_gather x1, blocking collectives, per_device(): whole = lax.all_gather(latents, 'neuron', axis=1, tiled=True)  22.8 us
    unnamed x7, local copies, waits for them, and re-layouts  15.4 us
    lt x16, other arithmetic, accumulate(): resid = jnp.where((bins < length)[None, :], jnp.exp(eta) - observed, 0.0)  10.9 us
  transfers between devices with their start and end apart: 2, of which 2 were waited for; matrix products, arithmetic and copies ran while one was open for 0% of the time, Pallas kernels for 0%

profile of v2, /device:TPU:8, one launch (start us, length us, event | category | flops | bytes accessed | tf_op | source)
XLA Modules:
  0.0 255.4 jit_solution(5036521654585094453)
XLA Ops:
  7.9 22.8 %all_gather.9 = bf16[64,4096]{1,0:T(8,128)(2,1)S(1)} all-gather(bf16[64,256]{1,0:T(8,128)(2,1)} %param.9), channel_id=1, replica_groups=mesh['region'=16,'neuron'=16] {'neuron'}, dimensions={1}, use_global_device_ids=true | all-gather | bytes 557056 | tf_op jit(solution)/shard_map/all_gather | solution.py:71
  32.7 14.5 %copy.9 = bf16[1,1280,4096]{1,2,0:T(8,128)(2,1)} copy(bf16[1,1280,4096]{2,1,0:T(8,128)(2,1)} %param.8) | data formatting | bytes 20971520 | tf_op args[0]
  47.4 0.7 copy-done.1
  48.1 47.3 %while.18 = (s32[]{:T(128)}, f32[64,1280]{1,0:T(8,128)S(1)}, f32[1280]{0:T(1024)S(1)}, f32[64,4096]{1,0:T(8,128)S(1)}, bf16[64,4096]{1,0:T(8,128)(2,1)S(1)}, /*i...) while((s32[]{:T(128)}, f32[64,1280]{1,0:T(8,128)S(1)}, ...), condition=%wide.region_2.3_spmd.clone, body=%wide.region_0.2_spmd.clone.sunk | while | flops 127960832 | bytes 3776474 | solution.py:78
  48.8 1.6 fusion.44
  51.7 1.6 fusion.44
  54.7 1.6 fusion.44
  57.6 1.6 fusion.44
  60.6 1.6 fusion.44
  63.5 1.6 fusion.44
  66.5 1.6 fusion.44
  69.5 1.6 fusion.44
  72.4 1.6 fusion.44
  75.4 1.6 fusion.44
  78.3 1.6 fusion.44
  81.3 1.6 fusion.44
  84.3 1.6 fusion.44
  87.2 1.6 fusion.44
  90.2 1.6 fusion.44
  93.1 1.6 fusion.44
  99.3 1.2 slice_select_fusion
  100.6 76.1 %reduce-scatter.2.cloned.1.call-done = f32[64,256]{1,0:T(8,128)} async-done(((f32[64,4096]{1,0:T(8,128)}), f32[64,256]{1,0:T(8,128)}) %reduce-scatter.2.cloned.1.call-update) | async-done | bytes 65552 | tf_op jit(solution)/shard_map/reduce_scatter | solution.py:80
  177.3 69.3 %all-gather.3.cloned.1.call-done = f32[1024,256]{1,0:T(8,128)} async-done(((f32[64,256]{1,0:T(8,128)}), f32[1024,256]{1,0:T(8,128)}) %all-gather.3.cloned.1.call-update) | async-done | bytes 1048592 | tf_op jit(solution)/shard_map/all_gather | solution.py:8
  246.6 1.9 reduce_sum.22
  (119 shorter events, 27.9 us)
Async XLA Ops:
  7.2 169.5 %reduce-scatter.2.cloned.1.call-start = ((), (), s32[]{:S(2)}) async-start(), calls=%async_computation.1 | async-start | bytes 1114112 | tf_op jit(solution)/shard_map/reduce_scatter | solution.py:80
  47.2 0.9 copy-start.1
  47.2 0.9 copy-start.2
  95.4 0.8 copy-start
  100.6 146.1 %all-gather.3.cloned.1.call-start = ((), (), s32[]{:S(2)}) async-start(), calls=%async_computation.2 | async-start | bytes 1114112 | tf_op jit(solution)/shard_map/all_gather | solution.py:8
Sparse Core Ops, SparseCore 0:
  100.7 75.9 reduce-scatter.1
  178.6 67.9 all-gather.2
